TPU v7x, 32 devices: a whole 2x2x4 slice. The times are simulated.
32 devices in a mesh: kern: 4 (over x, core), slab: 8 (over z, y).
Axes of the slice: x: 2, y: 2, z: 4, core: 2. Of those that a mesh axis runs over, the one named last changes fastest.
Arguments:
- layout: int32 [4096, 4096], P('slab', 'kern'), may hold values 0 or 1
- band_freqs: int32 [128], replicated, may hold values from -256 to 255, as said below
- kernels: float32 [2, 48, 128, 128], P(None, 'kern'), may hold values from -6 to 6
- eigen_values: float32 [48], P('kern'), may hold values from 0.1 to 1
- bake_rates: float32 [5], replicated, may hold values from 0.1 to 0.25
Outputs:
- aerial_image: float32 [4096, 4096], P('slab', 'kern')
- latent_acid: float32 [4096, 4096], P('slab', 'kern')
Inputs may be any that keep to these rules, and one draw needn't show every extreme that they name: `band_freqs`: the 128 numbers are distinct; both ends of the range are among them.
All inputs are finite; a program needn't handle non-finite values. No bound on the sum of `layout` on one device may be relied on, other than what follows from the above.
Results may differ from a plain program's by a relative error of at most 0.0017.
Values sent between devices are 32-bit elements; how exact they have to be, the bound alone decides.
A program may use at most 128 MiB of HBM per device.

v0:
```python
import math

import jax
import jax.numpy as jnp
from jax import lax
from jax.sharding import PartitionSpec as P

N = 4096
W = 128
FIELDS = 48
STEPS = 2


highest = lax.Precision.HIGHEST


def padded_2(cells, sides, width):
    for axis, dim in sides:
        count = lax.axis_size(axis)
        head = lax.slice_in_dim(cells, 0, width, axis=dim)
        tail = lax.slice_in_dim(cells, cells.shape[dim] - width, cells.shape[dim], axis=dim)
        cells = jnp.concatenate(
            [
                lax.ppermute(tail, axis, [(i, (i + 1) % count) for i in range(count)]),
                cells,
                lax.ppermute(head, axis, [((i + 1) % count, i) for i in range(count)]),
            ],
            axis=dim,
        )
    return cells


def tables(frequencies, first_index, length):
    positions = first_index + jnp.arange(length, dtype=jnp.int32)
    angles = jnp.mod(positions[:, None] * frequencies[None, :], N).astype(jnp.float32) * (
        2.0 * math.pi / N
    )
    return (jnp.cos(angles), jnp.sin(angles))


def stencil(padded):
    centre = padded[:, 1:-1, 1:-1]
    return (
        padded[:, 2:, 1:-1]
        + padded[:, :-2, 1:-1]
        + padded[:, 1:-1, 2:]
        + padded[:, 1:-1, :-2]
        - 4.0 * centre
    )


def bake(aerial_image, bake_rates, extend):
    dill_rate, acid_rate, quench_rate, react_rate, quench_start = (
        bake_rates[0],
        bake_rates[1],
        bake_rates[2],
        bake_rates[3],
        bake_rates[4],
    )
    acid_field = 1.0 - jnp.exp(-4.0 * dill_rate * aerial_image)
    acid_diffusion = acid_rate * (0.5 + 0.5 * acid_field)
    quencher = jnp.zeros_like(acid_field) + quench_start
    for bake_step in range(STEPS):
        laplaces = stencil(extend(jnp.stack([acid_field, quencher])))
        reaction = 4.0 * react_rate * acid_field * quencher
        new_acid = acid_field + acid_diffusion * laplaces[0] - reaction
        quencher = quencher + quench_rate * laplaces[1] - reaction
        acid_field = new_acid
    return acid_field


def shards(layout, band_freqs, kernels, eigen_values, bake_rates):
    rows = layout.shape[0]
    cols = layout.shape[1]
    row_first = lax.axis_index("slab") * rows
    col_first = lax.axis_index("kern") * cols
    transmit = (2 * layout - 1).astype(jnp.float32)
    cos_col, sin_col = tables(band_freqs, col_first, cols)
    along_re = jnp.dot(transmit, cos_col, precision=highest)
    along_im = -jnp.dot(transmit, sin_col, precision=highest)
    cos_row, sin_row = tables(band_freqs, row_first, rows)
    first = (
        jnp.dot(cos_row.T, along_re, precision=highest)
        + jnp.dot(sin_row.T, along_im, precision=highest)
    ) / N
    second = (
        jnp.dot(cos_row.T, along_im, precision=highest)
        - jnp.dot(sin_row.T, along_re, precision=highest)
    ) / N
    spectrum = lax.psum(jnp.stack([first, second]), ("kern", "slab"))
    spec_re = spectrum[0]
    spec_im = spectrum[1]
    row_table = jnp.concatenate([cos_row, sin_row], 1).astype(jnp.bfloat16)
    cos_all, sin_all = tables(band_freqs, 0, N)
    col_table = jnp.concatenate(
        [jnp.concatenate([cos_all.T, sin_all.T], 1), jnp.concatenate([-sin_all.T, cos_all.T], 1)], 0
    ).astype(jnp.bfloat16)

    def one_field(total_sum, field_item):
        kern_re, kern_im, eigen_one = field_item
        prod_re = spec_re * kern_re - spec_im * kern_im
        prod_im = spec_re * kern_im + spec_im * kern_re
        spectral_block = jnp.concatenate(
            [jnp.concatenate([prod_re, prod_im], 1), jnp.concatenate([-prod_im, prod_re], 1)], 0
        ).astype(jnp.bfloat16)
        row_field = (
            jnp.dot(row_table, spectral_block, preferred_element_type=jnp.float32) / W
        ).astype(jnp.bfloat16)
        field_pair = jnp.dot(row_field, col_table, preferred_element_type=jnp.float32)
        power = field_pair[:, :N] * field_pair[:, :N] + field_pair[:, N:] * field_pair[:, N:]
        return (total_sum + eigen_one * power, None)

    partial_sum, unused = lax.scan(
        one_field, jnp.zeros((rows, N), jnp.float32), (kernels[0], kernels[1], eigen_values)
    )
    aerial_image = lax.psum_scatter(partial_sum, "kern", scatter_dimension=1, tiled=True) / FIELDS

    def extend_grid(stacked):
        return padded_2(stacked, (("slab", 1), ("kern", 2)), 1)

    latent_acid = bake(aerial_image, bake_rates, extend_grid)
    return (aerial_image, latent_acid)


def solution(mesh):
    return jax.shard_map(
        shards,
        mesh=mesh,
        in_specs=(P("slab", "kern"), P(), P(None, "kern", None, None), P("kern"), P()),
        out_specs=(P("slab", "kern"), P("slab", "kern")),
        check_vma=False,
    )
```

profile of v0, /device:TPU:0, one launch (start us, length us, event | category | flops | bytes accessed | tf_op | source)
XLA Modules:
  0.0 606.7 jit_solution(6149603116685291674)
XLA Ops:
  7.2 5.5 fusion.54
  25.1 9.0 %fusion.66 = (bf16[128,4096]{1,0:T(8,128)(2,1)S(1)}, bf16[128,4096]{1,0:T(8,128)(2,1)S(1)}, bf16[128,4096]{1,0:T(8,128)(2,1)S(1)}) fusion(s32[128]{0:T(128)S(1)} %copy-done.6), kind=kLoop, calls=%fused_computation.103 | loop fusion | flops 9437184 | bytes 3146240 | tf_op jit(solution)/shard_map/convert.11
  36.8 18.6 %maximum_maximum_fusion = bf16[256,8192]{1,0:T(8,128)(2,1)} fusion(bf16[128,4096]{1,0:T(8,128)(2,1)S(1)} %get-tuple-element.129, bf16[128,4096]{1,0:T(8,128)(2,1)S(1)} %get-tuple-element.128, bf16[128,4096]{1,0:T(8,128)(2,1)S(1)} %get-tuple-element.127), kind=kLoop, calls=%fused_computation.44 | loop fusion | flops 16777216 | bytes 7340032 | tf_op jit(solution)/shard_map/concatenate | solution.py:95
  55.4 93.7 %all-reduce.3.cloned.1.call-done = f32[2,128,128]{2,1,0:T(8,128)} async-done(((f32[2,128,128]{2,1,0:T(8,128)}), f32[2,128,128]{2,1,0:T(8,128)}) %all-reduce.3.cloned.1.call-update) | async-done | bytes 131088 | tf_op jit(solution)/shard_map/psum | solution.py:90
  150.0 296.3 %while.11 = (s32[]{:T(128)}, f32[512,4096]{1,0:T(8,128)}, f32[12]{0:T(128)S(1)}, f32[12,128,128]{2,1,0:T(8,128)}, f32[128,128]{1,0:T(8,128)S(1)}, /*index=5*/f32...) while((s32[]{:T(128)}, f32[512,4096]{1,0:T(8,128)}, ...), condition=%wide.region_2.3_spmd.clone, body=%wide.region_1.2_spmd.clone.sunk | while | flops 2228125696 | bytes 55378056 | solution.py:113
  151.1 9.5 %fusion.142 = f32[512,8192]{1,0:T(8,128)} fusion(bf16[256,8192]{1,0:T(8,128)(2,1)} %get-tuple-element.221, bf16[512,256]{1,0:T(8,128)(2,1)S(1)} %get-tuple-element.220, bf16[128,128]{1,0:T(8,128)(2,1)S(1)} %get-tuple-element.188, bf16[128,128]{1,0:T(8,128)(2,1)S(1)} %negate_convert_fusion.3, bf16[128,128]{1,0:T(8,128)(2,1)S(1)} %get-tuple-element.190), kind=kOutput, calls=%fused_computation.7.clone.1 | convolution fusion | flops 2215378944 | bytes 21331968 | tf_op jit(solution)/shard_map/while/body/eval_jaxpr/dot_general | solution.py:109
  161.2 10.1 %fusion.143 = f32[512,4096]{1,0:T(8,128)} fusion(f32[512,8192]{1,0:T(8,128)} %fusion.142, f32[512,4096]{1,0:T(8,128)} %get-tuple-element.203, f32[]{:T(128)} %bitcast.79, pred[]{:T(512)S(6)} %compare.7), kind=kLoop, calls=%fused_computation.3.clone.1 | loop fusion | flops 12582912 | bytes 33554436 | tf_op jit(solution)/shard_map/while/body/eval_jaxpr/add | solution.py:111
  172.2 9.5 %fusion.142 = f32[512,8192]{1,0:T(8,128)} fusion(bf16[256,8192]{1,0:T(8,128)(2,1)} %get-tuple-element.221, bf16[512,256]{1,0:T(8,128)(2,1)S(1)} %get-tuple-element.220, bf16[128,128]{1,0:T(8,128)(2,1)S(1)} %get-tuple-element.188, bf16[128,128]{1,0:T(8,128)(2,1)S(1)} %negate_convert_fusion.3, bf16[128,128]{1,0:T(8,128)(2,1)S(1)} %get-tuple-element.190), kind=kOutput, calls=%fused_computation.7.clone.1 | convolution fusion | flops 2215378944 | bytes 21331968 | tf_op jit(solution)/shard_map/while/body/eval_jaxpr/dot_general | solution.py:109
  182.3 14.0 %fusion.143 = f32[512,4096]{1,0:T(8,128)} fusion(f32[512,8192]{1,0:T(8,128)} %fusion.142, f32[512,4096]{1,0:T(8,128)} %get-tuple-element.203, f32[]{:T(128)} %bitcast.79, pred[]{:T(512)S(6)} %compare.7), kind=kLoop, calls=%fused_computation.3.clone.1 | loop fusion | flops 12582912 | bytes 33554436 | tf_op jit(solution)/shard_map/while/body/eval_jaxpr/add | solution.py:111
  197.2 9.5 %fusion.142 = f32[512,8192]{1,0:T(8,128)} fusion(bf16[256,8192]{1,0:T(8,128)(2,1)} %get-tuple-element.221, bf16[512,256]{1,0:T(8,128)(2,1)S(1)} %get-tuple-element.220, bf16[128,128]{1,0:T(8,128)(2,1)S(1)} %get-tuple-element.188, bf16[128,128]{1,0:T(8,128)(2,1)S(1)} %negate_convert_fusion.3, bf16[128,128]{1,0:T(8,128)(2,1)S(1)} %get-tuple-element.190), kind=kOutput, calls=%fused_computation.7.clone.1 | convolution fusion | flops 2215378944 | bytes 21331968 | tf_op jit(solution)/shard_map/while/body/eval_jaxpr/dot_general | solution.py:109
  207.3 14.0 %fusion.143 = f32[512,4096]{1,0:T(8,128)} fusion(f32[512,8192]{1,0:T(8,128)} %fusion.142, f32[512,4096]{1,0:T(8,128)} %get-tuple-element.203, f32[]{:T(128)} %bitcast.79, pred[]{:T(512)S(6)} %compare.7), kind=kLoop, calls=%fused_computation.3.clone.1 | loop fusion | flops 12582912 | bytes 33554436 | tf_op jit(solution)/shard_map/while/body/eval_jaxpr/add | solution.py:111
  222.2 9.5 %fusion.142 = f32[512,8192]{1,0:T(8,128)} fusion(bf16[256,8192]{1,0:T(8,128)(2,1)} %get-tuple-element.221, bf16[512,256]{1,0:T(8,128)(2,1)S(1)} %get-tuple-element.220, bf16[128,128]{1,0:T(8,128)(2,1)S(1)} %get-tuple-element.188, bf16[128,128]{1,0:T(8,128)(2,1)S(1)} %negate_convert_fusion.3, bf16[128,128]{1,0:T(8,128)(2,1)S(1)} %get-tuple-element.190), kind=kOutput, calls=%fused_computation.7.clone.1 | convolution fusion | flops 2215378944 | bytes 21331968 | tf_op jit(solution)/shard_map/while/body/eval_jaxpr/dot_general | solution.py:109
  232.3 14.0 %fusion.143 = f32[512,4096]{1,0:T(8,128)} fusion(f32[512,8192]{1,0:T(8,128)} %fusion.142, f32[512,4096]{1,0:T(8,128)} %get-tuple-element.203, f32[]{:T(128)} %bitcast.79, pred[]{:T(512)S(6)} %compare.7), kind=kLoop, calls=%fused_computation.3.clone.1 | loop fusion | flops 12582912 | bytes 33554436 | tf_op jit(solution)/shard_map/while/body/eval_jaxpr/add | solution.py:111
  247.2 9.5 %fusion.142 = f32[512,8192]{1,0:T(8,128)} fusion(bf16[256,8192]{1,0:T(8,128)(2,1)} %get-tuple-element.221, bf16[512,256]{1,0:T(8,128)(2,1)S(1)} %get-tuple-element.220, bf16[128,128]{1,0:T(8,128)(2,1)S(1)} %get-tuple-element.188, bf16[128,128]{1,0:T(8,128)(2,1)S(1)} %negate_convert_fusion.3, bf16[128,128]{1,0:T(8,128)(2,1)S(1)} %get-tuple-element.190), kind=kOutput, calls=%fused_computation.7.clone.1 | convolution fusion | flops 2215378944 | bytes 21331968 | tf_op jit(solution)/shard_map/while/body/eval_jaxpr/dot_general | solution.py:109
  257.3 14.0 %fusion.143 = f32[512,4096]{1,0:T(8,128)} fusion(f32[512,8192]{1,0:T(8,128)} %fusion.142, f32[512,4096]{1,0:T(8,128)} %get-tuple-element.203, f32[]{:T(128)} %bitcast.79, pred[]{:T(512)S(6)} %compare.7), kind=kLoop, calls=%fused_computation.3.clone.1 | loop fusion | flops 12582912 | bytes 33554436 | tf_op jit(solution)/shard_map/while/body/eval_jaxpr/add | solution.py:111
  272.2 9.5 %fusion.142 = f32[512,8192]{1,0:T(8,128)} fusion(bf16[256,8192]{1,0:T(8,128)(2,1)} %get-tuple-element.221, bf16[512,256]{1,0:T(8,128)(2,1)S(1)} %get-tuple-element.220, bf16[128,128]{1,0:T(8,128)(2,1)S(1)} %get-tuple-element.188, bf16[128,128]{1,0:T(8,128)(2,1)S(1)} %negate_convert_fusion.3, bf16[128,128]{1,0:T(8,128)(2,1)S(1)} %get-tuple-element.190), kind=kOutput, calls=%fused_computation.7.clone.1 | convolution fusion | flops 2215378944 | bytes 21331968 | tf_op jit(solution)/shard_map/while/body/eval_jaxpr/dot_general | solution.py:109
  282.3 14.0 %fusion.143 = f32[512,4096]{1,0:T(8,128)} fusion(f32[512,8192]{1,0:T(8,128)} %fusion.142, f32[512,4096]{1,0:T(8,128)} %get-tuple-element.203, f32[]{:T(128)} %bitcast.79, pred[]{:T(512)S(6)} %compare.7), kind=kLoop, calls=%fused_computation.3.clone.1 | loop fusion | flops 12582912 | bytes 33554436 | tf_op jit(solution)/shard_map/while/body/eval_jaxpr/add | solution.py:111
  297.2 9.5 %fusion.142 = f32[512,8192]{1,0:T(8,128)} fusion(bf16[256,8192]{1,0:T(8,128)(2,1)} %get-tuple-element.221, bf16[512,256]{1,0:T(8,128)(2,1)S(1)} %get-tuple-element.220, bf16[128,128]{1,0:T(8,128)(2,1)S(1)} %get-tuple-element.188, bf16[128,128]{1,0:T(8,128)(2,1)S(1)} %negate_convert_fusion.3, bf16[128,128]{1,0:T(8,128)(2,1)S(1)} %get-tuple-element.190), kind=kOutput, calls=%fused_computation.7.clone.1 | convolution fusion | flops 2215378944 | bytes 21331968 | tf_op jit(solution)/shard_map/while/body/eval_jaxpr/dot_general | solution.py:109
  307.3 14.0 %fusion.143 = f32[512,4096]{1,0:T(8,128)} fusion(f32[512,8192]{1,0:T(8,128)} %fusion.142, f32[512,4096]{1,0:T(8,128)} %get-tuple-element.203, f32[]{:T(128)} %bitcast.79, pred[]{:T(512)S(6)} %compare.7), kind=kLoop, calls=%fused_computation.3.clone.1 | loop fusion | flops 12582912 | bytes 33554436 | tf_op jit(solution)/shard_map/while/body/eval_jaxpr/add | solution.py:111
  322.2 9.5 %fusion.142 = f32[512,8192]{1,0:T(8,128)} fusion(bf16[256,8192]{1,0:T(8,128)(2,1)} %get-tuple-element.221, bf16[512,256]{1,0:T(8,128)(2,1)S(1)} %get-tuple-element.220, bf16[128,128]{1,0:T(8,128)(2,1)S(1)} %get-tuple-element.188, bf16[128,128]{1,0:T(8,128)(2,1)S(1)} %negate_convert_fusion.3, bf16[128,128]{1,0:T(8,128)(2,1)S(1)} %get-tuple-element.190), kind=kOutput, calls=%fused_computation.7.clone.1 | convolution fusion | flops 2215378944 | bytes 21331968 | tf_op jit(solution)/shard_map/while/body/eval_jaxpr/dot_general | solution.py:109
  332.3 14.0 %fusion.143 = f32[512,4096]{1,0:T(8,128)} fusion(f32[512,8192]{1,0:T(8,128)} %fusion.142, f32[512,4096]{1,0:T(8,128)} %get-tuple-element.203, f32[]{:T(128)} %bitcast.79, pred[]{:T(512)S(6)} %compare.7), kind=kLoop, calls=%fused_computation.3.clone.1 | loop fusion | flops 12582912 | bytes 33554436 | tf_op jit(solution)/shard_map/while/body/eval_jaxpr/add | solution.py:111
  347.2 9.5 %fusion.142 = f32[512,8192]{1,0:T(8,128)} fusion(bf16[256,8192]{1,0:T(8,128)(2,1)} %get-tuple-element.221, bf16[512,256]{1,0:T(8,128)(2,1)S(1)} %get-tuple-element.220, bf16[128,128]{1,0:T(8,128)(2,1)S(1)} %get-tuple-element.188, bf16[128,128]{1,0:T(8,128)(2,1)S(1)} %negate_convert_fusion.3, bf16[128,128]{1,0:T(8,128)(2,1)S(1)} %get-tuple-element.190), kind=kOutput, calls=%fused_computation.7.clone.1 | convolution fusion | flops 2215378944 | bytes 21331968 | tf_op jit(solution)/shard_map/while/body/eval_jaxpr/dot_general | solution.py:109
  357.2 14.0 %fusion.143 = f32[512,4096]{1,0:T(8,128)} fusion(f32[512,8192]{1,0:T(8,128)} %fusion.142, f32[512,4096]{1,0:T(8,128)} %get-tuple-element.203, f32[]{:T(128)} %bitcast.79, pred[]{:T(512)S(6)} %compare.7), kind=kLoop, calls=%fused_computation.3.clone.1 | loop fusion | flops 12582912 | bytes 33554436 | tf_op jit(solution)/shard_map/while/body/eval_jaxpr/add | solution.py:111
  372.2 9.5 %fusion.142 = f32[512,8192]{1,0:T(8,128)} fusion(bf16[256,8192]{1,0:T(8,128)(2,1)} %get-tuple-element.221, bf16[512,256]{1,0:T(8,128)(2,1)S(1)} %get-tuple-element.220, bf16[128,128]{1,0:T(8,128)(2,1)S(1)} %get-tuple-element.188, bf16[128,128]{1,0:T(8,128)(2,1)S(1)} %negate_convert_fusion.3, bf16[128,128]{1,0:T(8,128)(2,1)S(1)} %get-tuple-element.190), kind=kOutput, calls=%fused_computation.7.clone.1 | convolution fusion | flops 2215378944 | bytes 21331968 | tf_op jit(solution)/shard_map/while/body/eval_jaxpr/dot_general | solution.py:109
  382.2 14.0 %fusion.143 = f32[512,4096]{1,0:T(8,128)} fusion(f32[512,8192]{1,0:T(8,128)} %fusion.142, f32[512,4096]{1,0:T(8,128)} %get-tuple-element.203, f32[]{:T(128)} %bitcast.79, pred[]{:T(512)S(6)} %compare.7), kind=kLoop, calls=%fused_computation.3.clone.1 | loop fusion | flops 12582912 | bytes 33554436 | tf_op jit(solution)/shard_map/while/body/eval_jaxpr/add | solution.py:111
  397.1 9.5 %fusion.142 = f32[512,8192]{1,0:T(8,128)} fusion(bf16[256,8192]{1,0:T(8,128)(2,1)} %get-tuple-element.221, bf16[512,256]{1,0:T(8,128)(2,1)S(1)} %get-tuple-element.220, bf16[128,128]{1,0:T(8,128)(2,1)S(1)} %get-tuple-element.188, bf16[128,128]{1,0:T(8,128)(2,1)S(1)} %negate_convert_fusion.3, bf16[128,128]{1,0:T(8,128)(2,1)S(1)} %get-tuple-element.190), kind=kOutput, calls=%fused_computation.7.clone.1 | convolution fusion | flops 2215378944 | bytes 21331968 | tf_op jit(solution)/shard_map/while/body/eval_jaxpr/dot_general | solution.py:109
  407.2 14.0 %fusion.143 = f32[512,4096]{1,0:T(8,128)} fusion(f32[512,8192]{1,0:T(8,128)} %fusion.142, f32[512,4096]{1,0:T(8,128)} %get-tuple-element.203, f32[]{:T(128)} %bitcast.79, pred[]{:T(512)S(6)} %compare.7), kind=kLoop, calls=%fused_computation.3.clone.1 | loop fusion | flops 12582912 | bytes 33554436 | tf_op jit(solution)/shard_map/while/body/eval_jaxpr/add | solution.py:111
  422.1 9.5 %fusion.142 = f32[512,8192]{1,0:T(8,128)} fusion(bf16[256,8192]{1,0:T(8,128)(2,1)} %get-tuple-element.221, bf16[512,256]{1,0:T(8,128)(2,1)S(1)} %get-tuple-element.220, bf16[128,128]{1,0:T(8,128)(2,1)S(1)} %get-tuple-element.188, bf16[128,128]{1,0:T(8,128)(2,1)S(1)} %negate_convert_fusion.3, bf16[128,128]{1,0:T(8,128)(2,1)S(1)} %get-tuple-element.190), kind=kOutput, calls=%fused_computation.7.clone.1 | convolution fusion | flops 2215378944 | bytes 21331968 | tf_op jit(solution)/shard_map/while/body/eval_jaxpr/dot_general | solution.py:109
  432.2 14.0 %fusion.143 = f32[512,4096]{1,0:T(8,128)} fusion(f32[512,8192]{1,0:T(8,128)} %fusion.142, f32[512,4096]{1,0:T(8,128)} %get-tuple-element.203, f32[]{:T(128)} %bitcast.79, pred[]{:T(512)S(6)} %compare.7), kind=kLoop, calls=%fused_computation.3.clone.1 | loop fusion | flops 12582912 | bytes 33554436 | tf_op jit(solution)/shard_map/while/body/eval_jaxpr/add | solution.py:111
  448.1 69.0 %reduce-scatter.2.cloned.1.call-done = f32[512,1024]{1,0:T(8,128)} async-done(((f32[512,4096]{1,0:T(8,128)}), f32[512,1024]{1,0:T(8,128)}) %reduce-scatter.2.cloned.1.call-update) | async-done | bytes 2097168 | tf_op jit(solution)/shard_map/reduce_scatter | solution.py:116
  537.0 29.4 %fusion.27 = f32[2,512,1024]{2,0,1:T(2,128)S(1)} fusion(f32[2,514,1]{2,0,1:T(2,128)S(1)} %copy.26, f32[2,1,1024]{2,0,1:T(2,128)S(1)} %collective-permute-done, f32[2,512,1024]{2,0,1:T(2,128)} %copy-done, f32[2,1,1024]{2,0,1:T(2,128)S(1)} %collective-permute-done.1, f32[2,514,1]{2,0,1:T(2,128)S(1)} %copy.24), kind=kLoop, calls=%fused_computation.34 | loop fusion | flops 13631488 | bytes 8413216 | tf_op jit(solution)/shard_map/sub | solution.py:44
  587.3 12.1 %fusion.43 = f32[512,1024]{1,0:T(8,128)} fusion(f32[1,512,1024]{2,1,0:T(8,128)} %copy-done.1, f32[1,512,1024]{2,1,0:T(8,128)S(1)} %get-tuple-element.111, f32[2,514,1]{2,1,0:T(8,128)S(1)} %copy.38, f32[2,514,1]{2,1,0:T(8,128)S(1)} %copy.36, f32[2,1,1024]{2,1,0:T(1,128)S(1)} %copy.30, f32[2,1,1024]{2,1,0:T(1,128)S(1)} %copy.32, f32[]{:T(128)} %bitcast.9, ...), kind=kLoop, calls=%fused_computation.61 | loop fusion | flops 17825792 | bytes 12607536 | tf_op jit(solution)/shard_map/sub | solution.py:66
  (109 shorter events, 75.0 us)
Async XLA Ops:
  7.2 5.6 copy-start.7
  7.2 5.6 copy-start.6
  7.2 141.9 %all-reduce.3.cloned.1.call-start = ((), (), s32[]{:S(2)}) async-start(), calls=%async_computation.1 | async-start | bytes 262144 | tf_op jit(solution)/shard_map/psum | solution.py:90
  23.8 493.4 %reduce-scatter.2.cloned.1.call-start = ((), (), s32[]{:S(2)}) async-start(), calls=%async_computation.2 | async-start | bytes 10485760 | tf_op jit(solution)/shard_map/reduce_scatter | solution.py:116
  36.8 113.2 %copy-start.8 = (f32[12]{0:T(128)S(1)}, f32[12]{0:T(128)}, u32[]{:S(2)}) copy-start(f32[12]{0:T(128)} %param.10) | copy-start | bytes 148
  446.2 0.7 copy-start.5
  521.7 6.3 %collective-permute-start = (f32[2,1,1024]{2,0,1:T(2,128)S(1)}, f32[2,1,1024]{2,0,1:T(2,128)S(1)}, u32[]{:S(2)}, u32[]{:S(2)}) collective-permute-start(f32[2,1,1024]{2,0,1:T(2,128)S(1)} %get-tuple-element.115), channel_id=1, source_target_pairs={{1,0},{2,1},{3,2},{4,3},{5,4},{6,5},{7,6},{0,7},{9,8},{10,9},{11,1... | collective-permute-start | bytes 24584 | tf_op jit(solution)/shard_map/ppermute | solution.py:26
  526.0 6.3 %collective-permute-start.1 = (f32[2,1,1024]{2,0,1:T(2,128)S(1)}, f32[2,1,1024]{2,0,1:T(2,128)S(1)}, u32[]{:S(2)}, u32[]{:S(2)}) collective-permute-start(f32[2,1,1024]{2,0,1:T(2,128)S(1)} %get-tuple-element.114), channel_id=1, source_target_pairs={{0,1},{1,2},{2,3},{3,4},{4,5},{5,6},{6,7},{7,0},{8,9},{9,10},{10,1... | collective-permute-start | bytes 24584 | tf_op jit(solution)/shard_map/ppermute | solution.py:24
  528.0 5.1 copy-start
  533.4 1.4 collective-permute-start.2
  533.7 3.1 collective-permute-start.3
  566.4 4.9 copy-start.4
  571.3 4.1 copy-start.2
  571.3 4.1 copy-start.3
  575.3 8.0 %copy-start.1 = (f32[1,512,1024]{2,1,0:T(8,128)}, f32[1,512,1024]{2,1,0:T(8,128)S(1)}, u32[]{:S(2)}) copy-start(f32[1,512,1024]{2,1,0:T(8,128)S(1)} %get-tuple-element.113) | copy-start | bytes 6291460
  575.4 3.7 collective-permute-start.4
  577.0 6.3 %collective-permute-start.5 = (f32[2,1,1024]{2,0,1:T(2,128)S(1)}, f32[2,1,1024]{2,0,1:T(2,128)S(1)}, u32[]{:S(2)}, u32[]{:S(2)}) collective-permute-start(f32[2,1,1024]{2,0,1:T(2,128)S(1)} %copy.31), channel_id=1, source_target_pairs={{0,1},{1,2},{2,3},{3,4},{4,5},{5,6},{6,7},{7,0},{8,9},{9,10},{10,1... | collective-permute-start | bytes 24584 | tf_op jit(solution)/shard_map/ppermute | solution.py:24
  583.8 1.4 collective-permute-start.6
  584.0 3.1 collective-permute-start.7
Sparse Core Ops, SparseCore 0:
  23.9 125.1 all-reduce.2
  446.4 70.7 reduce-scatter.1
where the time goes:
time: 617 us; the launch traced here: 607 us
  other arithmetic  258 us (42%)
  waiting for transfers between devices  177 us (29%)
  matrix products  130 us (21%)
  local copies, waits for them, and re-layouts  18.5 us (3%)
  between operations  16.1 us (3%)
  starting transfers between devices  7.54 us (1%)
    add x12, other arithmetic, one_field(): return (total_sum + eigen_one * power, None)  164 us
    dot_general x12, matrix products, one_field(): jnp.dot(row_field, col_table, preferred_element_type=jnp.float32)  114 us
    psum x1, waiting for transfers between devices, shards(): spectrum = lax.psum(jnp.stack([first, second]), ('kern', 'slab'))  93.7 us
    reduce_scatter x1, waiting for transfers between devices, shards(): lax.psum_scatter(partial_sum, 'kern', scatter_dimension=1, tiled=True)  69 us
    sub x1, other arithmetic, stencil(): padded[:, 2:, 1:-1] + padded[:, :-2, 1:-1] + padded[:, 1:-1, 2:]  29.4 us
    another operation x26, other arithmetic  21.1 us
    concatenate x1, other arithmetic, shards(): jnp.concatenate([jnp.concatenate([cos_all.T, sin_all.T], 1), jnp.concaten...  18.6 us
  transfers between devices with their start and end apart: 10, of which 8 were waited for; matrix products, arithmetic and copies ran while one was open for 6% of the time, Pallas kernels for 0%

commit v1 on v0

v1 whole, which is shorter than its diff:
```python
import functools
import math

import jax
import jax.numpy as jnp
import numpy as np
from jax import lax
from jax.experimental import pallas as pl
from jax.experimental.pallas import tpu as pltpu
from jax.sharding import PartitionSpec as P

BAND = 256
COARSE = 4 * BAND
HALO = 8
SIDE = 64
f32 = jnp.float32
bf16 = jnp.bfloat16


def trig(count, total):
    m = count & (total - 1)
    quarter = total // 4
    quad = (m + quarter // 2) >> (quarter.bit_length() - 1)
    rest = m - quad * quarter
    x = rest.astype(f32) * (2.0 * math.pi / total)
    y = x * x
    s = x * (1.0 + y * (-1.0 / 6 + y * (1.0 / 120 + y * (-1.0 / 5040 + y * (1.0 / 362880)))))
    c = 1.0 + y * (-0.5 + y * (1.0 / 24 + y * (-1.0 / 720 + y * (1.0 / 40320 + y * (-1.0 / 3628800)))))
    odd = (quad & 1) == 1
    cos = jnp.where(odd, s, c)
    sin = jnp.where(odd, c, s)
    cos = jnp.where(((quad + 1) & 2) == 2, -cos, cos)
    sin = jnp.where((quad & 2) == 2, -sin, sin)
    return cos, sin


def split(a):
    hi = a.astype(bf16)
    return hi, (a - hi.astype(f32)).astype(bf16)


def dot(a, b):
    return jnp.dot(a, b, preferred_element_type=f32)


def row_chunk(ext):
    return max(c for c in range(16, 97, 16) if ext % c == 0)


def image_kernel(
    n_kern, n_slab, layout_ref, frow_ref, fcol_ref, kern_ref, eig_ref, out_ref,
    kb, colw, rowt_h, rowt_l, rowb, ct, part, recv_a, recv_b, spec, rf, acc, recv_s,
    send_k, recv_k, send_a, rsem_a, send_b, rsem_b, send_c, rsem_c, send_s, rsem_s,
):
    rows, cols = layout_ref.shape
    n = cols * n_kern
    fields = kern_ref.shape[1]
    w = kern_ref.shape[2]
    half = n_kern // 2
    ext = rows + 2 * HALO
    piece = 2 * w // n_slab
    my_k = lax.axis_index("kern")
    my_s = lax.axis_index("slab")
    my_h = my_k // 2
    core = my_k % 2

    def slab_peer(d):
        return lax.rem(my_s + d, n_slab)

    def kern_peer(d):
        return lax.rem(my_k + d, n_kern)

    barrier = pltpu.get_barrier_semaphore()

    @pl.loop(1, n_slab)
    def _(d):
        pl.semaphore_signal(barrier, inc=1, device_id={"slab": slab_peer(d)}, device_id_type=pl.DeviceIdType.MESH)

    for d in range(1, n_kern):
        pl.semaphore_signal(barrier, inc=1, device_id={"kern": kern_peer(d)}, device_id_type=pl.DeviceIdType.MESH)

    for f in range(fields):
        for c in range(2):
            kb[my_h, f, c] = kern_ref[c, f] * eig_ref[f]
    pl.semaphore_wait(barrier, n_slab - 1 + n_kern - 1)

    def kern_copy(d):
        return pltpu.make_async_remote_copy(
            src_ref=kb.at[my_h], dst_ref=kb.at[my_h],
            send_sem=send_k.at[d - 1], recv_sem=recv_k.at[d - 1],
            device_id={"kern": lax.rem(my_h + d, half) * 2 + core}, device_id_type=pl.DeviceIdType.MESH)

    for d in range(1, half):
        kern_copy(d).start()

    pos = my_k * cols + lax.broadcasted_iota(jnp.int32, (cols, w), 0)
    cos, sin = trig(pos * frow_ref[...], n)
    ch, cl = split(cos)
    sh, sl = split(sin)
    colw[:, 0:w] = ch
    colw[:, w:2 * w] = sh
    colw[:, 2 * w:3 * w] = cl
    colw[:, 3 * w:4 * w] = sl
    pos = my_s * rows + lax.broadcasted_iota(jnp.int32, (w, rows), 1)
    cos, sin = trig(pos * fcol_ref[...], n)
    ch, cl = split(cos)
    sh, sl = split(sin)
    rowt_h[0:w] = ch
    rowt_h[w:2 * w] = sh
    rowt_l[0:w] = cl
    rowt_l[w:2 * w] = sl
    x = (2 * layout_ref[...] - 1).astype(f32).astype(bf16)
    along = dot(x, colw[...])
    ah, al = split(along[:, :2 * w] + along[:, 2 * w:])
    both = dot(rowt_h[...], ah) + (dot(rowt_h[...], al) + dot(rowt_l[...], ah))
    re = (both[:w, :w] - both[w:, w:]) * (1.0 / n)
    im = (both[:w, w:] + both[w:, :w]) * (-1.0 / n)
    full = jnp.concatenate([re, im], 0)
    for i in range(n_slab):
        part[i] = full[i * piece:(i + 1) * piece]

    def copy_a(d):
        return pltpu.make_async_remote_copy(
            src_ref=part.at[slab_peer(d)], dst_ref=recv_a.at[d - 1],
            send_sem=send_a.at[d - 1], recv_sem=rsem_a.at[d - 1],
            device_id={"slab": slab_peer(d)}, device_id_type=pl.DeviceIdType.MESH)

    @pl.loop(1, n_slab)
    def _(d):
        copy_a(d).start()

    r = lax.broadcasted_iota(jnp.int32, (ext, w), 0)
    pos = my_s * rows + jnp.where(r < rows + HALO, r, r - ext)
    cos, sin = trig(pos * frow_ref[...], n)
    rowb[:, 0:w] = cos.astype(bf16)
    rowb[:, w:2 * w] = sin.astype(bf16)
    block = COARSE // n_kern
    for j in range(n_kern):
        pos = (n // COARSE) * (j * block + lax.broadcasted_iota(jnp.int32, (w, block), 1))
        cos, sin = trig(pos * fcol_ref[...], n)
        ct[j, 0:w, 0:block] = cos.astype(bf16)
        ct[j, 0:w, block:2 * block] = sin.astype(bf16)
        ct[j, w:2 * w, 0:block] = (-sin).astype(bf16)
        ct[j, w:2 * w, block:2 * block] = cos.astype(bf16)

    @pl.loop(1, n_slab)
    def _(d):
        copy_a(d).wait()

    total = part[my_s]
    for d in range(1, n_slab):
        total = total + recv_a[d - 1]
    recv_b[my_k] = total

    def copy_b(d):
        return pltpu.make_async_remote_copy(
            src_ref=recv_b.at[my_k], dst_ref=recv_b.at[my_k],
            send_sem=send_b.at[d - 1], recv_sem=rsem_b.at[d - 1],
            device_id={"kern": kern_peer(d)}, device_id_type=pl.DeviceIdType.MESH)

    for d in range(1, n_kern):
        copy_b(d).start()
    for d in range(1, n_kern):
        copy_b(d).wait()
    total = recv_b[0]
    for k in range(1, n_kern):
        total = total + recv_b[k]
    spec[my_s] = total

    def copy_c(d):
        return pltpu.make_async_remote_copy(
            src_ref=spec.at[my_s], dst_ref=spec.at[my_s],
            send_sem=send_c.at[d - 1], recv_sem=rsem_c.at[d - 1],
            device_id={"slab": slab_peer(d)}, device_id_type=pl.DeviceIdType.MESH)

    @pl.loop(1, n_slab)
    def _(d):
        copy_c(d).start()

    @pl.loop(1, n_slab)
    def _(d):
        copy_c(d).wait()

    for d in range(1, half):
        kern_copy(d).wait()

    full = jnp.concatenate([spec[i] for i in range(n_slab)], 0)
    spec_re = full[:w]
    spec_im = full[w:]
    step = row_chunk(ext)
    chunks = ext // step
    count = half * fields

    for h in range(half):
        @pl.loop(0, fields)
        def _(f):
            kr = kb[h, f, 0]
            ki = kb[h, f, 1]
            pr = (spec_re * kr - spec_im * ki)
            pi = (spec_re * ki + spec_im * kr)
            prod = jnp.concatenate(
                [jnp.concatenate([pr, pi], 1), jnp.concatenate([-pi, pr], 1)], 0).astype(bf16)
            field = (dot(rowb[...], prod) * (1.0 / w)).astype(bf16)
            at = pl.multiple_of((h * fields + f) * step, 16)
            for i in range(chunks):
                rf[i, pl.ds(at, step), :] = field[i * step:(i + 1) * step]

    partner = my_k + 1 - 2 * core

    def copy_s(j):
        return pltpu.make_async_remote_copy(
            src_ref=acc.at[j], dst_ref=recv_s.at[j],
            send_sem=send_s.at[j], recv_sem=rsem_s.at[j],
            device_id={"kern": partner}, device_id_type=pl.DeviceIdType.MESH)

    @pl.loop(0, n_kern)
    def _(j):
        @pl.loop(0, chunks)
        def _(i):
            e = dot(rf[i], ct[j])
            total = None
            for f in range(count):
                one = e[f * step:(f + 1) * step]
                sq = one * one
                sq = sq[:, :block] + sq[:, block:]
                total = sq if total is None else total + sq
            acc[j, pl.ds(pl.multiple_of(i * step, 16), step), :] = total

        copy_s(j).start()

    for j in range(n_kern):
        copy_s(j).wait()
        out_ref[lax.rem(j + n_kern - my_k, n_kern)] = acc[j] + recv_s[j]


def bake_kernel(fields, coarse_ref, dh_ref, dl_ref, rates_ref, aer_ref, lat_ref, xh, xl, aer, acid0, acid1):
    n_kern, ext, block = coarse_ref.shape
    rows, cols = aer_ref.shape
    wide = dh_ref.shape[1]
    step = row_chunk(ext)
    chunks = ext // step
    dill, arate, react, qstart = rates_ref[0], rates_ref[1], rates_ref[3], rates_ref[4]
    for j in range(n_kern):
        hi, lo = split(coarse_ref[j])
        xh[:, j * block:(j + 1) * block] = hi
        xl[:, j * block:(j + 1) * block] = lo
    tile = 384 if wide % 384 == 0 else 128
    for c in range(0, wide, tile):
        s = slice(c, c + tile)
        aer[:, s] = (dot(xh[...], dh_ref[:, s]) + (dot(xl[...], dh_ref[:, s]) + dot(xh[...], dl_ref[:, s]))) * (
            1.0 / fields)

    @pl.loop(0, chunks)
    def _(i):
        at = pl.ds(pl.multiple_of(i * step, 16), step)
        acid0[at, :] = 1.0 - jnp.exp((-4.0 * dill) * aer[at, :])

    aer_ref[...] = aer[0:rows, 0:cols]

    def laplace(ref, i):
        first = i * step
        mid = ref[pl.ds(pl.multiple_of(first, 8), step), :]
        before = ref[pl.ds(pl.multiple_of(lax.rem(first + ext - 8, ext), 8), 8), :]
        after = ref[pl.ds(pl.multiple_of(lax.rem(first + step, ext), 8), 8), :]
        tall = jnp.concatenate([before, mid, after], 0)
        up = pltpu.roll(tall, 1, 0)[8:8 + step]
        down = pltpu.roll(tall, step + 15, 0)[8:8 + step]
        left = pltpu.roll(mid, 1, 1)
        right = pltpu.roll(mid, wide - 1, 1)
        return mid, down + up + right + left - 4.0 * mid

    @pl.loop(0, chunks)
    def _(i):
        mid, lap = laplace(acid0, i)
        value = mid + (arate * (0.5 + 0.5 * mid)) * lap - 4.0 * react * mid * qstart
        acid1[pl.ds(pl.multiple_of(i * step, 16), step), :] = value

    @pl.loop(0, chunks)
    def _(i):
        at = pl.ds(pl.multiple_of(i * step, 16), step)
        mid, lap = laplace(acid1, i)
        first = acid0[at, :]
        quench = qstart - 4.0 * react * first * qstart
        aer[at, :] = mid + (arate * (0.5 + 0.5 * first)) * lap - 4.0 * react * mid * quench

    lat_ref[...] = aer[0:rows, 0:cols]


def interpolation(cols, n):
    wide = cols + 2 * SIDE
    c = np.arange(wide)
    c = np.where(c < cols + SIDE, c, c - wide)
    ratio = n // COARSE
    t = c[None, :] - ratio * np.arange(COARSE)[:, None]
    zero = t % n == 0
    safe = np.where(zero, 1, t)
    d = np.sin(np.pi * (safe % (2 * ratio)) / ratio) / (COARSE * np.tan(np.pi * safe / n))
    d = np.where(zero, 1.0, np.where(t % ratio == 0, 0.0, d))
    hi = d.astype(jnp.bfloat16)
    lo = (d - hi.astype(np.float64)).astype(jnp.bfloat16)
    return hi, lo


def shards(n_kern, n_slab, layout, band_freqs, kernels, eigen_values, bake_rates):
    rows, cols = layout.shape
    fields, w = kernels.shape[1], kernels.shape[2]
    n = cols * n_kern
    ext = rows + 2 * HALO
    half = n_kern // 2
    block = COARSE // n_kern
    piece = 2 * w // n_slab
    step = row_chunk(ext)
    chunks = ext // step
    eig = jnp.broadcast_to(jnp.sqrt(eigen_values)[:, None, None], (fields, 1, w))
    vmem = pl.BlockSpec(memory_space=pltpu.VMEM)
    dma = pltpu.SemaphoreType.DMA
    coarse = pl.pallas_call(
        functools.partial(image_kernel, n_kern, n_slab),
        out_shape=jax.ShapeDtypeStruct((n_kern, ext, block), f32),
        in_specs=[vmem] * 5,
        out_specs=vmem,
        scratch_shapes=[
            pltpu.VMEM((half, fields, 2, w, w), f32),
            pltpu.VMEM((cols, 4 * w), bf16),
            pltpu.VMEM((2 * w, rows), bf16),
            pltpu.VMEM((2 * w, rows), bf16),
            pltpu.VMEM((ext, 2 * w), bf16),
            pltpu.VMEM((n_kern, 2 * w, 2 * block), bf16),
            pltpu.VMEM((n_slab, piece, w), f32),
            pltpu.VMEM((n_slab - 1, piece, w), f32),
            pltpu.VMEM((n_kern, piece, w), f32),
            pltpu.VMEM((n_slab, piece, w), f32),
            pltpu.VMEM((chunks, half * fields * step, 2 * w), bf16),
            pltpu.VMEM((n_kern, ext, block), f32),
            pltpu.VMEM((n_kern, ext, block), f32),
            dma((half,)), dma((half,)),
            dma((n_slab - 1,)), dma((n_slab - 1,)),
            dma((n_kern - 1,)), dma((n_kern - 1,)),
            dma((n_slab - 1,)), dma((n_slab - 1,)),
            dma((n_kern,)), dma((n_kern,)),
        ],
        compiler_params=pltpu.CompilerParams(
            collective_id=0, has_side_effects=True, vmem_limit_bytes=56 * 2**20),
        name="coarse_image",
    )(layout, band_freqs.reshape(1, w), band_freqs.reshape(w, 1), kernels, eig)
    dh, dl = interpolation(cols, n)
    wide = cols + 2 * SIDE
    return pl.pallas_call(
        functools.partial(bake_kernel, fields * n_kern),
        out_shape=[jax.ShapeDtypeStruct((rows, cols), f32)] * 2,
        in_specs=[vmem, vmem, vmem, pl.BlockSpec(memory_space=pltpu.SMEM)],
        out_specs=[vmem, vmem],
        scratch_shapes=[
            pltpu.VMEM((ext, COARSE), bf16),
            pltpu.VMEM((ext, COARSE), bf16),
            pltpu.VMEM((ext, wide), f32),
            pltpu.VMEM((ext, wide), f32),
            pltpu.VMEM((ext, wide), f32),
        ],
        compiler_params=pltpu.CompilerParams(vmem_limit_bytes=56 * 2**20),
        name="interpolate_bake",
    )(coarse, jnp.asarray(dh), jnp.asarray(dl), bake_rates)


def solution(mesh):
    return jax.shard_map(
        functools.partial(shards, mesh.shape["kern"], mesh.shape["slab"]),
        mesh=mesh,
        in_specs=(P("slab", "kern"), P(), P(None, "kern", None, None), P("kern"), P()),
        out_specs=(P("slab", "kern"), P("slab", "kern")),
        check_vma=False,
    )
```

time: 617 us -> 96.8 us (0.16); the launches traced: 607 us -> 96.6 us
  other arithmetic: 258 us -> 0 us
  waiting for transfers between devices: 177 us -> 0 us
  matrix products: 130 us -> 0 us
  Pallas kernels: 0 us -> 93.2 us
  local copies, waits for them, and re-layouts: 18.5 us -> 2.73 us
  between operations: 16.1 us -> 0.64 us
  starting transfers between devices: 7.54 us -> 0 us
    add x15 -> x0, other arithmetic: 169 us -> none  [the longest x12 164 us: one_field(): return (total_sum + eigen_one * power, None)]
    dot_general x18 -> x0, matrix products: 130 us -> none  [the longest x12 114 us: one_field(): jnp.dot(row_field, col_table, preferred_element_type=jnp.float32)]
    psum x1 -> x0, waiting for transfers between devices: 93.7 us -> none  [shards(): spectrum = lax.psum(jnp.stack([first, second]), ('kern', 'slab'))]
    pallas_call x0 -> x2, Pallas kernels: none -> 93.2 us  [the longest x1 77.7 us: shards(): pl.pallas_call(functools.partial(image_kernel, n_kern, n_slab), out_shape...]
    reduce_scatter x1 -> x0, waiting for transfers between devices: 69 us -> none  [shards(): lax.psum_scatter(partial_sum, 'kern', scatter_dimension=1, tiled=True)]
    sub x2 -> x0, other arithmetic: 41.4 us -> none  [the longest x1 29.4 us: stencil(): padded[:, 2:, 1:-1] + padded[:, :-2, 1:-1] + padded[:, 1:-1, 2:]]
    another operation x30 -> x0, other arithmetic: 27.7 us -> none
    concatenate x2 -> x0, other arithmetic: 18.6 us -> none  [the longest x1 18.6 us: shards(): jnp.concatenate([jnp.concatenate([cos_all.T, sin_all.T], 1), jnp.concaten...]
  transfers between devices with their start and end apart: 10 -> 0, of which waited for: 8 -> 0; matrix products, arithmetic and copies ran while one was open for 6% -> 0% of each run, Pallas kernels for 0% -> 0%
where the time goes in v1:
time: 96.8 us; the launch traced here: 96.6 us
  Pallas kernels  93.2 us (96%)
  local copies, waits for them, and re-layouts  2.73 us (3%)
    pallas_call x1, Pallas kernels, shards(): pl.pallas_call(functools.partial(image_kernel, n_kern, n_slab), out_shape...  77.7 us
    pallas_call x1, Pallas kernels, shards(): pl.pallas_call(functools.partial(bake_kernel, fields * n_kern), out_shape...  15.6 us

profile of v1, /device:TPU:0, one launch (start us, length us, event | category | flops | bytes accessed | tf_op | source)
XLA Modules:
  0.0 96.6 jit_solution(15208453040371296921)
XLA Ops:
  0.6 0.7 sqrt.3
  1.3 0.7 broadcast_in_dim.2.eig_ref
  2.0 1.4 %copy.9.fcol_ref = s32[128,1]{1,0:T(8,128)} copy(s32[128,1]{0,1:T(1,128)} %bitcast.2) | data formatting | bytes 1024 | tf_op jit(solution)/shard_map/reshape | solution.py:345
  3.4 77.7 %coarse_image.1.coarse_ref = f32[4,528,256]{2,1,0:T(8,128)} custom-call(s32[512,1024]{1,0:T(8,128)} %layout_ref.1, s32[1,128]{1,0:T(1,128)} %bitcast.3, s32[128,1]{1,0:T(8,128)} %copy.9.fcol_ref, f32[2,12,128,128]{3,2,1,0:T(8,128)} %kern_ref.1, f32[12,1,128]{2,1,0:T(1,128)} %broadcast_in_dim.2.eig_ref), custom_call_target="tpu_custom_call" | custom-call | tf_op jit(solution)/shard_map/coarse_image/pallas_call | solution.py:317
  81.0 15.6 %interpolate_bake.1 = (f32[512,1024]{1,0:T(8,128)}, f32[512,1024]{1,0:T(8,128)}) custom-call(f32[4,528,256]{2,1,0:T(8,128)} %coarse_image.1.coarse_ref, bf16[1024,1152]{1,0:T(8,128)(2,1)} %constant.4.clone.dh_ref, bf16[1024,1152]{1,0:T(8,128)(2,1)} %constant.5.clone.dl_ref, f32[5]{0:T(128)} %rates_ref.1), custom_call_target="tpu_custom_call" | custom-call | tf_op jit(solution)/shard_map/interpolate_bake/pallas_call | solution.py:348

commit v2 on v1

--- a/solution.py
+++ b/solution.py
@@ -48,7 +48,7 @@
 
 
 def image_kernel(
-    n_kern, n_slab, layout_ref, frow_ref, fcol_ref, kern_ref, eig_ref, out_ref,
+    n_kern, n_slab, layout_ref, frow_ref, kern_ref, eig_ref, out_ref,
     kb, colw, rowt_h, rowt_l, rowb, ct, part, recv_a, recv_b, spec, rf, acc, recv_s,
     send_k, recv_k, send_a, rsem_a, send_b, rsem_b, send_c, rsem_c, send_s, rsem_s,
 ):
@@ -80,8 +80,9 @@
         pl.semaphore_signal(barrier, inc=1, device_id={"kern": kern_peer(d)}, device_id_type=pl.DeviceIdType.MESH)
 
     for f in range(fields):
+        weight = jnp.sqrt(jnp.full((1, w), eig_ref[f], f32))
         for c in range(2):
-            kb[my_h, f, c] = kern_ref[c, f] * eig_ref[f]
+            kb[my_h, f, c] = kern_ref[c, f] * weight
     pl.semaphore_wait(barrier, n_slab - 1 + n_kern - 1)
 
     def kern_copy(d):
@@ -93,6 +94,7 @@
     for d in range(1, half):
         kern_copy(d).start()
 
+    fcol = jnp.transpose(jnp.broadcast_to(frow_ref[...], (w, w)))[:, 0:1]
     pos = my_k * cols + lax.broadcasted_iota(jnp.int32, (cols, w), 0)
     cos, sin = trig(pos * frow_ref[...], n)
     ch, cl = split(cos)
@@ -102,7 +104,7 @@
     colw[:, 2 * w:3 * w] = cl
     colw[:, 3 * w:4 * w] = sl
     pos = my_s * rows + lax.broadcasted_iota(jnp.int32, (w, rows), 1)
-    cos, sin = trig(pos * fcol_ref[...], n)
+    cos, sin = trig(pos * fcol, n)
     ch, cl = split(cos)
     sh, sl = split(sin)
     rowt_h[0:w] = ch
@@ -137,7 +139,7 @@
     block = COARSE // n_kern
     for j in range(n_kern):
         pos = (n // COARSE) * (j * block + lax.broadcasted_iota(jnp.int32, (w, block), 1))
-        cos, sin = trig(pos * fcol_ref[...], n)
+        cos, sin = trig(pos * fcol, n)
         ct[j, 0:w, 0:block] = cos.astype(bf16)
         ct[j, 0:w, block:2 * block] = sin.astype(bf16)
         ct[j, w:2 * w, 0:block] = (-sin).astype(bf16)
@@ -181,59 +183,60 @@
     def _(d):
         copy_c(d).wait()
 
-    for d in range(1, half):
-        kern_copy(d).wait()
-
     full = jnp.concatenate([spec[i] for i in range(n_slab)], 0)
     spec_re = full[:w]
     spec_im = full[w:]
     step = row_chunk(ext)
     chunks = ext // step
-    count = half * fields
-
-    for h in range(half):
+    partner = my_k + 1 - 2 * core
+
+    def copy_s(j):
+        return pltpu.make_async_remote_copy(
+            src_ref=acc.at[j], dst_ref=recv_s.at[j],
+            send_sem=send_s.at[j], recv_sem=rsem_s.at[j],
+            device_id={"kern": partner}, device_id_type=pl.DeviceIdType.MESH)
+
+    for phase in range(half):
+        h = lax.rem(my_h + half - phase, half)
+        if phase > 0:
+            kern_copy(phase).wait()
+
         @pl.loop(0, fields)
         def _(f):
             kr = kb[h, f, 0]
             ki = kb[h, f, 1]
-            pr = (spec_re * kr - spec_im * ki)
-            pi = (spec_re * ki + spec_im * kr)
+            pr = spec_re * kr - spec_im * ki
+            pi = spec_re * ki + spec_im * kr
             prod = jnp.concatenate(
                 [jnp.concatenate([pr, pi], 1), jnp.concatenate([-pi, pr], 1)], 0).astype(bf16)
             field = (dot(rowb[...], prod) * (1.0 / w)).astype(bf16)
-            at = pl.multiple_of((h * fields + f) * step, 16)
+            at = pl.multiple_of(f * step, 16)
             for i in range(chunks):
                 rf[i, pl.ds(at, step), :] = field[i * step:(i + 1) * step]
 
-    partner = my_k + 1 - 2 * core
-
-    def copy_s(j):
-        return pltpu.make_async_remote_copy(
-            src_ref=acc.at[j], dst_ref=recv_s.at[j],
-            send_sem=send_s.at[j], recv_sem=rsem_s.at[j],
-            device_id={"kern": partner}, device_id_type=pl.DeviceIdType.MESH)
-
-    @pl.loop(0, n_kern)
-    def _(j):
-        @pl.loop(0, chunks)
-        def _(i):
-            e = dot(rf[i], ct[j])
-            total = None
-            for f in range(count):
-                one = e[f * step:(f + 1) * step]
-                sq = one * one
-                sq = sq[:, :block] + sq[:, block:]
-                total = sq if total is None else total + sq
-            acc[j, pl.ds(pl.multiple_of(i * step, 16), step), :] = total
-
-        copy_s(j).start()
+        @pl.loop(0, n_kern)
+        def _(j):
+            @pl.loop(0, chunks)
+            def _(i):
+                at = pl.ds(pl.multiple_of(i * step, 16), step)
+                e = dot(rf[i], ct[j])
+                total = None if phase == 0 else acc[j, at, :]
+                for f in range(fields):
+                    one = e[f * step:(f + 1) * step]
+                    sq = one * one
+                    sq = sq[:, :block] + sq[:, block:]
+                    total = sq if total is None else total + sq
+                acc[j, at, :] = total
+
+            if phase == half - 1:
+                copy_s(j).start()
 
     for j in range(n_kern):
         copy_s(j).wait()
         out_ref[lax.rem(j + n_kern - my_k, n_kern)] = acc[j] + recv_s[j]
 
 
-def bake_kernel(fields, coarse_ref, dh_ref, dl_ref, rates_ref, aer_ref, lat_ref, xh, xl, aer, acid0, acid1):
+def bake_kernel(fields, coarse_ref, dh_ref, dl_ref, rates_ref, aer_ref, lat_ref, xs, aer, acid0, acid1):
     n_kern, ext, block = coarse_ref.shape
     rows, cols = aer_ref.shape
     wide = dh_ref.shape[1]
@@ -242,18 +245,15 @@
     dill, arate, react, qstart = rates_ref[0], rates_ref[1], rates_ref[3], rates_ref[4]
     for j in range(n_kern):
         hi, lo = split(coarse_ref[j])
-        xh[:, j * block:(j + 1) * block] = hi
-        xl[:, j * block:(j + 1) * block] = lo
+        xs[0:ext, j * block:(j + 1) * block] = hi
+        xs[ext:2 * ext, j * block:(j + 1) * block] = lo
     tile = 384 if wide % 384 == 0 else 128
     for c in range(0, wide, tile):
         s = slice(c, c + tile)
-        aer[:, s] = (dot(xh[...], dh_ref[:, s]) + (dot(xl[...], dh_ref[:, s]) + dot(xh[...], dl_ref[:, s]))) * (
-            1.0 / fields)
-
-    @pl.loop(0, chunks)
-    def _(i):
-        at = pl.ds(pl.multiple_of(i * step, 16), step)
-        acid0[at, :] = 1.0 - jnp.exp((-4.0 * dill) * aer[at, :])
+        both = dot(xs[...], dh_ref[:, s])
+        value = (both[:ext] + (both[ext:] + dot(xs[0:ext, :], dl_ref[:, s]))) * (1.0 / fields)
+        aer[:, s] = value
+        acid0[:, s] = 1.0 - jnp.exp((-4.0 * dill) * value)
 
     aer_ref[...] = aer[0:rows, 0:cols]
 
@@ -311,13 +311,12 @@
     piece = 2 * w // n_slab
     step = row_chunk(ext)
     chunks = ext // step
-    eig = jnp.broadcast_to(jnp.sqrt(eigen_values)[:, None, None], (fields, 1, w))
     vmem = pl.BlockSpec(memory_space=pltpu.VMEM)
     dma = pltpu.SemaphoreType.DMA
     coarse = pl.pallas_call(
         functools.partial(image_kernel, n_kern, n_slab),
         out_shape=jax.ShapeDtypeStruct((n_kern, ext, block), f32),
-        in_specs=[vmem] * 5,
+        in_specs=[vmem, vmem, vmem, pl.BlockSpec(memory_space=pltpu.SMEM)],
         out_specs=vmem,
         scratch_shapes=[
             pltpu.VMEM((half, fields, 2, w, w), f32),
@@ -330,7 +329,7 @@
             pltpu.VMEM((n_slab - 1, piece, w), f32),
             pltpu.VMEM((n_kern, piece, w), f32),
             pltpu.VMEM((n_slab, piece, w), f32),
-            pltpu.VMEM((chunks, half * fields * step, 2 * w), bf16),
+            pltpu.VMEM((chunks, fields * step, 2 * w), bf16),
             pltpu.VMEM((n_kern, ext, block), f32),
             pltpu.VMEM((n_kern, ext, block), f32),
             dma((half,)), dma((half,)),
@@ -340,9 +339,9 @@
             dma((n_kern,)), dma((n_kern,)),
         ],
         compiler_params=pltpu.CompilerParams(
-            collective_id=0, has_side_effects=True, vmem_limit_bytes=56 * 2**20),
+            collective_id=0, has_side_effects=True, vmem_limit_bytes=34 * 2**20),
         name="coarse_image",
-    )(layout, band_freqs.reshape(1, w), band_freqs.reshape(w, 1), kernels, eig)
+    )(layout, band_freqs.reshape(1, w), kernels, eigen_values)
     dh, dl = interpolation(cols, n)
     wide = cols + 2 * SIDE
     return pl.pallas_call(
@@ -351,13 +350,12 @@
         in_specs=[vmem, vmem, vmem, pl.BlockSpec(memory_space=pltpu.SMEM)],
         out_specs=[vmem, vmem],
         scratch_shapes=[
-            pltpu.VMEM((ext, COARSE), bf16),
-            pltpu.VMEM((ext, COARSE), bf16),
+            pltpu.VMEM((2 * ext, COARSE), bf16),
             pltpu.VMEM((ext, wide), f32),
             pltpu.VMEM((ext, wide), f32),
             pltpu.VMEM((ext, wide), f32),
         ],
-        compiler_params=pltpu.CompilerParams(vmem_limit_bytes=56 * 2**20),
+        compiler_params=pltpu.CompilerParams(vmem_limit_bytes=34 * 2**20),
         name="interpolate_bake",
     )(coarse, jnp.asarray(dh), jnp.asarray(dl), bake_rates)
 

time: 96.8 us -> 99.3 us (1.026)
  local copies, waits for them, and re-layouts: 2.73 us -> 4.31 us
    unnamed x0 -> x14, local copies, waits for them, and re-layouts: none -> 4.31 us
    pallas_call x1, Pallas kernels: 77.7 us -> 81.5 us  [shards(): pl.pallas_call(functools.partial(image_kernel, n_kern, n_slab), out_shape...]
    pallas_call x1, Pallas kernels: 15.6 us -> 12.6 us  [shards(): pl.pallas_call(functools.partial(bake_kernel, fields * n_kern), out_shape...]
    reshape x1 -> x0, local copies, waits for them, and re-layouts: 1.39 us -> none  [shards(): band_freqs.reshape(w, 1)]
where the time goes in v2:
time: 99.3 us; the launch traced here: 99.1 us
  Pallas kernels  94.1 us (95%)
  local copies, waits for them, and re-layouts  4.31 us (4%)
    pallas_call x1, Pallas kernels, shards(): pl.pallas_call(functools.partial(image_kernel, n_kern, n_slab), out_shape...  81.5 us
    pallas_call x1, Pallas kernels, shards(): pl.pallas_call(functools.partial(bake_kernel, fields * n_kern), out_shape...  12.6 us
    unnamed x14, local copies, waits for them, and re-layouts  4.31 us

profile of v2, /device:TPU:0, one launch (start us, length us, event | category | flops | bytes accessed | tf_op | source)
XLA Modules:
  0.0 99.1 jit_solution(16277847528041512144)
XLA Ops:
  0.6 0.0 copy-start.2
  0.6 1.6 %copy-done.2 = s32[512,1024]{1,0:T(8,128)S(1)} copy-done((s32[512,1024]{1,0:T(8,128)S(1)}, s32[512,1024]{1,0:T(8,128)}, u32[]{:S(2)}) %copy-start.2) | copy-done | bytes 2097176
  2.2 0.0 copy-start.3
  2.2 1.4 %copy-done.3 = f32[2,12,128,128]{3,2,1,0:T(8,128)S(1)} copy-done((f32[2,12,128,128]{3,2,1,0:T(8,128)S(1)}, f32[2,12,128,128]{3,2,1,0:T(8,128)}, u32[]{:S(2)}) %copy-start.3) | copy-done | bytes 1572888
  3.6 0.0 copy-start.4
  3.6 0.7 copy-done.4
  4.3 0.0 copy-start.5
  4.3 0.7 copy-done.5
  4.9 0.0 copy-start
  4.9 0.0 copy-start.1
  4.9 0.0 copy-start.6
  4.9 81.5 %coarse_image.1.coarse_ref = f32[4,528,256]{2,1,0:T(8,128)S(1)} custom-call(s32[512,1024]{1,0:T(8,128)S(1)} %copy-done.2, s32[1,128]{1,0:T(1,128)S(1)} %bitcast.1, f32[2,12,128,128]{3,2,1,0:T(8,128)S(1)} %copy-done.3, f32[12]{0:T(128)S(1)} %copy-done.5), custom_call_target="tpu_custom_call" | custom-call | tf_op jit(solution)/shard_map/coarse_image/pallas_call | solution.py:316
  86.5 0.0 copy-done
  86.5 0.0 copy-done.1
  86.5 0.0 copy-done.6
  86.5 12.6 %interpolate_bake.1 = (f32[512,1024]{1,0:T(8,128)}, f32[512,1024]{1,0:T(8,128)}) custom-call(f32[4,528,256]{2,1,0:T(8,128)S(1)} %coarse_image.1.coarse_ref, bf16[1024,1152]{1,0:T(8,128)(2,1)S(1)} %copy-done.1, bf16[1024,1152]{1,0:T(8,128)(2,1)S(1)} %copy-done, f32[5]{0:T(128)S(1)} %copy-done.6), custom_call_target="tpu_custom_call" | custom-call | tf_op jit(solution)/shard_map/interpolate_bake/pallas_call | solution.py:347
Async XLA Ops:
  0.6 1.6 %copy-start.2 = (s32[512,1024]{1,0:T(8,128)S(1)}, s32[512,1024]{1,0:T(8,128)}, u32[]{:S(2)}) copy-start(s32[512,1024]{1,0:T(8,128)} %layout_ref.1) | copy-start | bytes 6291460
  2.2 1.4 %copy-start.3 = (f32[2,12,128,128]{3,2,1,0:T(8,128)S(1)}, f32[2,12,128,128]{3,2,1,0:T(8,128)}, u32[]{:S(2)}) copy-start(f32[2,12,128,128]{3,2,1,0:T(8,128)} %kern_ref.1) | copy-start | bytes 4718596
  3.6 0.7 copy-start.4
  4.3 0.7 copy-start.5
  4.9 81.6 %copy-start = (bf16[1024,1152]{1,0:T(8,128)(2,1)S(1)}, bf16[1024,1152]{1,0:T(8,128)(2,1)}, u32[]{:S(2)}) copy-start(bf16[1024,1152]{1,0:T(8,128)(2,1)} %constant.5.clone.dl_ref) | copy-start | bytes 7077892
  4.9 81.6 %copy-start.1 = (bf16[1024,1152]{1,0:T(8,128)(2,1)S(1)}, bf16[1024,1152]{1,0:T(8,128)(2,1)}, u32[]{:S(2)}) copy-start(bf16[1024,1152]{1,0:T(8,128)(2,1)} %constant.4.clone.dh_ref) | copy-start | bytes 7077892
  4.9 81.6 %copy-start.6 = (f32[5]{0:T(128)S(1)}, f32[5]{0:T(128)}, u32[]{:S(2)}) copy-start(f32[5]{0:T(128)} %rates_ref.1) | copy-start | bytes 64

commit v3 on v2

--- a/solution.py
+++ b/solution.py
@@ -43,15 +43,19 @@
     return jnp.dot(a, b, preferred_element_type=f32)
 
 
-def row_chunk(ext):
-    return max(c for c in range(16, 97, 16) if ext % c == 0)
+def row_chunk(ext, most):
+    return max(c for c in range(16, most + 1, 16) if ext % c == 0)
 
 
 def image_kernel(
-    n_kern, n_slab, layout_ref, frow_ref, kern_ref, eig_ref, out_ref,
-    kb, colw, rowt_h, rowt_l, rowb, ct, part, recv_a, recv_b, spec, rf, acc, recv_s,
+    n_kern, n_slab, layout_hbm, frow_ref, kern_hbm, eig_ref, out_ref,
+    layout_ref, kern_ref, in_sem, kb, colw, rowt_h, rowt_l, rowb, ct, part, recv_a, recv_b, spec, rf, acc, recv_s,
     send_k, recv_k, send_a, rsem_a, send_b, rsem_b, send_c, rsem_c, send_s, rsem_s,
 ):
+    layout_in = pltpu.make_async_copy(layout_hbm, layout_ref, in_sem.at[0])
+    kern_in = pltpu.make_async_copy(kern_hbm, kern_ref, in_sem.at[1])
+    kern_in.start()
+    layout_in.start()
     rows, cols = layout_ref.shape
     n = cols * n_kern
     fields = kern_ref.shape[1]
@@ -79,6 +83,7 @@
     for d in range(1, n_kern):
         pl.semaphore_signal(barrier, inc=1, device_id={"kern": kern_peer(d)}, device_id_type=pl.DeviceIdType.MESH)
 
+    kern_in.wait()
     for f in range(fields):
         weight = jnp.sqrt(jnp.full((1, w), eig_ref[f], f32))
         for c in range(2):
@@ -111,6 +116,7 @@
     rowt_h[w:2 * w] = sh
     rowt_l[0:w] = cl
     rowt_l[w:2 * w] = sl
+    layout_in.wait()
     x = (2 * layout_ref[...] - 1).astype(f32).astype(bf16)
     along = dot(x, colw[...])
     ah, al = split(along[:, :2 * w] + along[:, 2 * w:])
@@ -186,7 +192,7 @@
     full = jnp.concatenate([spec[i] for i in range(n_slab)], 0)
     spec_re = full[:w]
     spec_im = full[w:]
-    step = row_chunk(ext)
+    step = row_chunk(ext, 192)
     chunks = ext // step
     partner = my_k + 1 - 2 * core
 
@@ -201,7 +207,7 @@
         if phase > 0:
             kern_copy(phase).wait()
 
-        @pl.loop(0, fields)
+        @pl.loop(0, fields, unroll=3)
         def _(f):
             kr = kb[h, f, 0]
             ki = kb[h, f, 1]
@@ -240,7 +246,7 @@
     n_kern, ext, block = coarse_ref.shape
     rows, cols = aer_ref.shape
     wide = dh_ref.shape[1]
-    step = row_chunk(ext)
+    step = row_chunk(ext, 96)
     chunks = ext // step
     dill, arate, react, qstart = rates_ref[0], rates_ref[1], rates_ref[3], rates_ref[4]
     for j in range(n_kern):
@@ -309,16 +315,20 @@
     half = n_kern // 2
     block = COARSE // n_kern
     piece = 2 * w // n_slab
-    step = row_chunk(ext)
+    step = row_chunk(ext, 192)
     chunks = ext // step
     vmem = pl.BlockSpec(memory_space=pltpu.VMEM)
+    anyw = pl.BlockSpec(memory_space=pl.ANY)
     dma = pltpu.SemaphoreType.DMA
     coarse = pl.pallas_call(
         functools.partial(image_kernel, n_kern, n_slab),
         out_shape=jax.ShapeDtypeStruct((n_kern, ext, block), f32),
-        in_specs=[vmem, vmem, vmem, pl.BlockSpec(memory_space=pltpu.SMEM)],
+        in_specs=[anyw, vmem, anyw, pl.BlockSpec(memory_space=pltpu.SMEM)],
         out_specs=vmem,
         scratch_shapes=[
+            pltpu.VMEM((rows, cols), jnp.int32),
+            pltpu.VMEM((2, fields, w, w), f32),
+            dma((2,)),
             pltpu.VMEM((half, fields, 2, w, w), f32),
             pltpu.VMEM((cols, 4 * w), bf16),
             pltpu.VMEM((2 * w, rows), bf16),
@@ -339,7 +349,7 @@
             dma((n_kern,)), dma((n_kern,)),
         ],
         compiler_params=pltpu.CompilerParams(
-            collective_id=0, has_side_effects=True, vmem_limit_bytes=34 * 2**20),
+            collective_id=0, has_side_effects=True, vmem_limit_bytes=56 * 2**20),
         name="coarse_image",
     )(layout, band_freqs.reshape(1, w), kernels, eigen_values)
     dh, dl = interpolation(cols, n)

time: 99.3 us -> 86.3 us (0.87)
  Pallas kernels: 94.1 us -> 83.9 us
  local copies, waits for them, and re-layouts: 4.31 us -> 1.62 us
    pallas_call x1, Pallas kernels: 81.5 us -> 71.3 us  [shards(): pl.pallas_call(functools.partial(image_kernel, n_kern, n_slab), out_shape...]
    unnamed x14 -> x8, local copies, waits for them, and re-layouts: 4.31 us -> 1.62 us
where the time goes in v3:
time: 86.3 us; the launch traced here: 86.2 us
  Pallas kernels  83.9 us (97%)
  local copies, waits for them, and re-layouts  1.62 us (2%)
    pallas_call x1, Pallas kernels, shards(): pl.pallas_call(functools.partial(image_kernel, n_kern, n_slab), out_shape...  71.3 us
    pallas_call x1, Pallas kernels, shards(): pl.pallas_call(functools.partial(bake_kernel, fields * n_kern), out_shape...  12.6 us

profile of v3, /device:TPU:0, one launch (start us, length us, event | category | flops | bytes accessed | tf_op | source)
XLA Modules:
  0.0 86.2 jit_solution(16516612482198771518)
XLA Ops:
  0.6 0.0 copy-start.1
  0.6 0.0 copy-start.2
  0.7 0.0 copy-start.3
  0.7 71.3 %coarse_image.1.coarse_ref = f32[4,528,256]{2,1,0:T(8,128)} custom-call(s32[512,1024]{1,0:T(8,128)} %layout_hbm.1, s32[1,128]{1,0:T(1,128)} %bitcast.1, f32[2,12,128,128]{3,2,1,0:T(8,128)} %kern_hbm.1, f32[12]{0:T(128)} %eig_ref.1), custom_call_target="tpu_custom_call" | custom-call | tf_op jit(solution)/shard_map/coarse_image/pallas_call | solution.py:323
  72.0 0.0 copy-done.1
  72.0 0.0 copy-done.2
  72.0 0.0 copy-done.3
  72.0 0.0 copy-start
  72.0 1.6 %copy-done = f32[4,528,256]{2,1,0:T(8,128)S(1)} copy-done((f32[4,528,256]{2,1,0:T(8,128)S(1)}, f32[4,528,256]{2,1,0:T(8,128)}, u32[]{:S(2)}) %copy-start) | copy-done | bytes 2162712
  73.6 12.6 %interpolate_bake.1 = (f32[512,1024]{1,0:T(8,128)}, f32[512,1024]{1,0:T(8,128)}) custom-call(f32[4,528,256]{2,1,0:T(8,128)S(1)} %copy-done, bf16[1024,1152]{1,0:T(8,128)(2,1)S(1)} %copy-done.2, bf16[1024,1152]{1,0:T(8,128)(2,1)S(1)} %copy-done.1, f32[5]{0:T(128)S(1)} %copy-done.3), custom_call_target="tpu_custom_call" | custom-call | tf_op jit(solution)/shard_map/interpolate_bake/pallas_call | solution.py:357
Async XLA Ops:
  0.6 71.4 %copy-start.1 = (bf16[1024,1152]{1,0:T(8,128)(2,1)S(1)}, bf16[1024,1152]{1,0:T(8,128)(2,1)}, u32[]{:S(2)}) copy-start(bf16[1024,1152]{1,0:T(8,128)(2,1)} %constant.5.clone.dl_ref) | copy-start | bytes 7077892
  0.6 71.4 %copy-start.2 = (bf16[1024,1152]{1,0:T(8,128)(2,1)S(1)}, bf16[1024,1152]{1,0:T(8,128)(2,1)}, u32[]{:S(2)}) copy-start(bf16[1024,1152]{1,0:T(8,128)(2,1)} %constant.4.clone.dh_ref) | copy-start | bytes 7077892
  0.7 71.3 %copy-start.3 = (f32[5]{0:T(128)S(1)}, f32[5]{0:T(128)}, u32[]{:S(2)}) copy-start(f32[5]{0:T(128)} %rates_ref.1) | copy-start | bytes 64
  72.0 1.6 %copy-start = (f32[4,528,256]{2,1,0:T(8,128)S(1)}, f32[4,528,256]{2,1,0:T(8,128)}, u32[]{:S(2)}) copy-start(f32[4,528,256]{2,1,0:T(8,128)} %coarse_image.1.coarse_ref) | copy-start | bytes 6488068

commit v4 on v3

--- a/solution.py
+++ b/solution.py
@@ -90,14 +90,17 @@
             kb[my_h, f, c] = kern_ref[c, f] * weight
     pl.semaphore_wait(barrier, n_slab - 1 + n_kern - 1)
 
-    def kern_copy(d):
+    early = fields // 4
+
+    def kern_copy(d, late):
+        some = pl.ds(early, fields - early) if late else pl.ds(0, early)
         return pltpu.make_async_remote_copy(
-            src_ref=kb.at[my_h], dst_ref=kb.at[my_h],
-            send_sem=send_k.at[d - 1], recv_sem=recv_k.at[d - 1],
+            src_ref=kb.at[my_h, some], dst_ref=kb.at[my_h, some],
+            send_sem=send_k.at[late, d - 1], recv_sem=recv_k.at[late, d - 1],
             device_id={"kern": lax.rem(my_h + d, half) * 2 + core}, device_id_type=pl.DeviceIdType.MESH)
 
     for d in range(1, half):
-        kern_copy(d).start()
+        kern_copy(d, 0).start()
 
     fcol = jnp.transpose(jnp.broadcast_to(frow_ref[...], (w, w)))[:, 0:1]
     pos = my_k * cols + lax.broadcasted_iota(jnp.int32, (cols, w), 0)
@@ -170,6 +173,8 @@
         copy_b(d).start()
     for d in range(1, n_kern):
         copy_b(d).wait()
+    for d in range(1, half):
+        kern_copy(d, 1).start()
     total = recv_b[0]
     for k in range(1, n_kern):
         total = total + recv_b[k]
@@ -205,7 +210,8 @@
     for phase in range(half):
         h = lax.rem(my_h + half - phase, half)
         if phase > 0:
-            kern_copy(phase).wait()
+            kern_copy(phase, 0).wait()
+            kern_copy(phase, 1).wait()
 
         @pl.loop(0, fields, unroll=3)
         def _(f):
@@ -242,9 +248,9 @@
         out_ref[lax.rem(j + n_kern - my_k, n_kern)] = acc[j] + recv_s[j]
 
 
-def bake_kernel(fields, coarse_ref, dh_ref, dl_ref, rates_ref, aer_ref, lat_ref, xs, aer, acid0, acid1):
+def bake_kernel(fields, coarse_ref, dh_ref, dl_ref, rates_ref, aer_hbm, lat_hbm, xs, aer, acid0, acid1, lat, sem):
     n_kern, ext, block = coarse_ref.shape
-    rows, cols = aer_ref.shape
+    rows, cols = aer_hbm.shape
     wide = dh_ref.shape[1]
     step = row_chunk(ext, 96)
     chunks = ext // step
@@ -261,10 +267,10 @@
         aer[:, s] = value
         acid0[:, s] = 1.0 - jnp.exp((-4.0 * dill) * value)
 
-    aer_ref[...] = aer[0:rows, 0:cols]
-
-    def laplace(ref, i):
-        first = i * step
+    aer_out = pltpu.make_async_copy(aer.at[0:rows, 0:cols], aer_hbm, sem.at[0])
+    aer_out.start()
+
+    def laplace(ref, first, step):
         mid = ref[pl.ds(pl.multiple_of(first, 8), step), :]
         before = ref[pl.ds(pl.multiple_of(lax.rem(first + ext - 8, ext), 8), 8), :]
         after = ref[pl.ds(pl.multiple_of(lax.rem(first + step, ext), 8), 8), :]
@@ -277,19 +283,32 @@
 
     @pl.loop(0, chunks)
     def _(i):
-        mid, lap = laplace(acid0, i)
+        mid, lap = laplace(acid0, i * step, step)
         value = mid + (arate * (0.5 + 0.5 * mid)) * lap - 4.0 * react * mid * qstart
         acid1[pl.ds(pl.multiple_of(i * step, 16), step), :] = value
 
-    @pl.loop(0, chunks)
+    last = math.gcd(rows, 64)
+    parts = rows // last
+
+    def lat_out(i):
+        at = pl.ds(pl.multiple_of(i * last, 16), last)
+        return pltpu.make_async_copy(lat.at[at, :], lat_hbm.at[at, :], sem.at[1 + i])
+
+    @pl.loop(0, parts)
     def _(i):
-        at = pl.ds(pl.multiple_of(i * step, 16), step)
-        mid, lap = laplace(acid1, i)
+        at = pl.ds(pl.multiple_of(i * last, 16), last)
+        mid, lap = laplace(acid1, i * last, last)
         first = acid0[at, :]
         quench = qstart - 4.0 * react * first * qstart
-        aer[at, :] = mid + (arate * (0.5 + 0.5 * first)) * lap - 4.0 * react * mid * quench
-
-    lat_ref[...] = aer[0:rows, 0:cols]
+        value = mid + (arate * (0.5 + 0.5 * first)) * lap - 4.0 * react * mid * quench
+        lat[at, :] = value[:, 0:cols]
+        lat_out(i).start()
+
+    aer_out.wait()
+
+    @pl.loop(0, parts)
+    def _(i):
+        lat_out(i).wait()
 
 
 def interpolation(cols, n):
@@ -342,7 +361,7 @@
             pltpu.VMEM((chunks, fields * step, 2 * w), bf16),
             pltpu.VMEM((n_kern, ext, block), f32),
             pltpu.VMEM((n_kern, ext, block), f32),
-            dma((half,)), dma((half,)),
+            dma((2, half)), dma((2, half)),
             dma((n_slab - 1,)), dma((n_slab - 1,)),
             dma((n_kern - 1,)), dma((n_kern - 1,)),
             dma((n_slab - 1,)), dma((n_slab - 1,)),
@@ -358,12 +377,14 @@
         functools.partial(bake_kernel, fields * n_kern),
         out_shape=[jax.ShapeDtypeStruct((rows, cols), f32)] * 2,
         in_specs=[vmem, vmem, vmem, pl.BlockSpec(memory_space=pltpu.SMEM)],
-        out_specs=[vmem, vmem],
+        out_specs=[anyw, anyw],
         scratch_shapes=[
             pltpu.VMEM((2 * ext, COARSE), bf16),
             pltpu.VMEM((ext, wide), f32),
             pltpu.VMEM((ext, wide), f32),
             pltpu.VMEM((ext, wide), f32),
+            pltpu.VMEM((rows, cols), f32),
+            dma((1 + rows // math.gcd(rows, 64),)),
         ],
         compiler_params=pltpu.CompilerParams(vmem_limit_bytes=34 * 2**20),
         name="interpolate_bake",

time: 86.3 us -> 72 us (0.83)
  Pallas kernels: 83.9 us -> 69.6 us
    pallas_call x1, Pallas kernels: 71.3 us -> 58.3 us  [shards(): pl.pallas_call(functools.partial(image_kernel, n_kern, n_slab), out_shape...]
    pallas_call x1, Pallas kernels: 12.6 us -> 11.2 us  [shards(): pl.pallas_call(functools.partial(bake_kernel, fields * n_kern), out_shape...]
where the time goes in v4:
time: 72 us; the launch traced here: 71.9 us
  Pallas kernels  69.6 us (97%)
  local copies, waits for them, and re-layouts  1.62 us (2%)
    pallas_call x1, Pallas kernels, shards(): pl.pallas_call(functools.partial(image_kernel, n_kern, n_slab), out_shape...  58.3 us
    pallas_call x1, Pallas kernels, shards(): pl.pallas_call(functools.partial(bake_kernel, fields * n_kern), out_shape...  11.2 us
    unnamed x8, local copies, waits for them, and re-layouts  1.62 us

profile of v4, /device:TPU:0, one launch (start us, length us, event | category | flops | bytes accessed | tf_op | source)
XLA Modules:
  0.0 71.9 jit_solution(18231068271816587351)
XLA Ops:
  0.6 0.0 copy-start.1
  0.6 0.0 copy-start.2
  0.7 0.0 copy-start.3
  0.7 58.3 %coarse_image.1.coarse_ref = f32[4,528,256]{2,1,0:T(8,128)} custom-call(s32[512,1024]{1,0:T(8,128)} %layout_hbm.1, s32[1,128]{1,0:T(1,128)} %bitcast.1, f32[2,12,128,128]{3,2,1,0:T(8,128)} %kern_hbm.1, f32[12]{0:T(128)} %eig_ref.1), custom_call_target="tpu_custom_call" | custom-call | tf_op jit(solution)/shard_map/coarse_image/pallas_call | solution.py:342
  59.0 0.0 copy-done.1
  59.0 0.0 copy-done.2
  59.0 0.0 copy-done.3
  59.0 0.0 copy-start
  59.0 1.6 %copy-done = f32[4,528,256]{2,1,0:T(8,128)S(1)} copy-done((f32[4,528,256]{2,1,0:T(8,128)S(1)}, f32[4,528,256]{2,1,0:T(8,128)}, u32[]{:S(2)}) %copy-start) | copy-done | bytes 2162712
  60.6 11.2 %interpolate_bake.1 = (f32[512,1024]{1,0:T(8,128)}, f32[512,1024]{1,0:T(8,128)}) custom-call(f32[4,528,256]{2,1,0:T(8,128)S(1)} %copy-done, bf16[1024,1152]{1,0:T(8,128)(2,1)S(1)} %copy-done.2, bf16[1024,1152]{1,0:T(8,128)(2,1)S(1)} %copy-done.1, f32[5]{0:T(128)S(1)} %copy-done.3), custom_call_target="tpu_custom_call" | custom-call | tf_op jit(solution)/shard_map/interpolate_bake/pallas_call | solution.py:376
Async XLA Ops:
  0.6 58.4 %copy-start.1 = (bf16[1024,1152]{1,0:T(8,128)(2,1)S(1)}, bf16[1024,1152]{1,0:T(8,128)(2,1)}, u32[]{:S(2)}) copy-start(bf16[1024,1152]{1,0:T(8,128)(2,1)} %constant.5.clone.dl_ref) | copy-start | bytes 7077892
  0.6 58.4 %copy-start.2 = (bf16[1024,1152]{1,0:T(8,128)(2,1)S(1)}, bf16[1024,1152]{1,0:T(8,128)(2,1)}, u32[]{:S(2)}) copy-start(bf16[1024,1152]{1,0:T(8,128)(2,1)} %constant.4.clone.dh_ref) | copy-start | bytes 7077892
  0.7 58.4 %copy-start.3 = (f32[5]{0:T(128)S(1)}, f32[5]{0:T(128)}, u32[]{:S(2)}) copy-start(f32[5]{0:T(128)} %rates_ref.1) | copy-start | bytes 64
  59.0 1.6 %copy-start = (f32[4,528,256]{2,1,0:T(8,128)S(1)}, f32[4,528,256]{2,1,0:T(8,128)}, u32[]{:S(2)}) copy-start(f32[4,528,256]{2,1,0:T(8,128)} %coarse_image.1.coarse_ref) | copy-start | bytes 6488068

commit v5 on v4

--- a/solution.py
+++ b/solution.py
@@ -88,9 +88,8 @@
         weight = jnp.sqrt(jnp.full((1, w), eig_ref[f], f32))
         for c in range(2):
             kb[my_h, f, c] = kern_ref[c, f] * weight
-    pl.semaphore_wait(barrier, n_slab - 1 + n_kern - 1)
-
-    early = fields // 4
+
+    early = fields // 3
 
     def kern_copy(d, late):
         some = pl.ds(early, fields - early) if late else pl.ds(0, early)
@@ -98,9 +97,6 @@
             src_ref=kb.at[my_h, some], dst_ref=kb.at[my_h, some],
             send_sem=send_k.at[late, d - 1], recv_sem=recv_k.at[late, d - 1],
             device_id={"kern": lax.rem(my_h + d, half) * 2 + core}, device_id_type=pl.DeviceIdType.MESH)
-
-    for d in range(1, half):
-        kern_copy(d, 0).start()
 
     fcol = jnp.transpose(jnp.broadcast_to(frow_ref[...], (w, w)))[:, 0:1]
     pos = my_k * cols + lax.broadcasted_iota(jnp.int32, (cols, w), 0)
@@ -111,6 +107,9 @@
     colw[:, w:2 * w] = sh
     colw[:, 2 * w:3 * w] = cl
     colw[:, 3 * w:4 * w] = sl
+    pl.semaphore_wait(barrier, n_slab - 1 + n_kern - 1)
+    for d in range(1, half):
+        kern_copy(d, 0).start()
     pos = my_s * rows + lax.broadcasted_iota(jnp.int32, (w, rows), 1)
     cos, sin = trig(pos * fcol, n)
     ch, cl = split(cos)
@@ -207,16 +206,18 @@
             send_sem=send_s.at[j], recv_sem=rsem_s.at[j],
             device_id={"kern": partner}, device_id_type=pl.DeviceIdType.MESH)
 
-    for phase in range(half):
+    groups = [(0, 0, fields)]
+    for phase in range(1, half):
+        groups += [(phase, 0, early), (phase, early, fields - early)]
+    for phase, first, some in groups:
         h = lax.rem(my_h + half - phase, half)
         if phase > 0:
-            kern_copy(phase, 0).wait()
-            kern_copy(phase, 1).wait()
-
-        @pl.loop(0, fields, unroll=3)
+            kern_copy(phase, int(first > 0)).wait()
+
+        @pl.loop(0, some, unroll=4)
         def _(f):
-            kr = kb[h, f, 0]
-            ki = kb[h, f, 1]
+            kr = kb[h, first + f, 0]
+            ki = kb[h, first + f, 1]
             pr = spec_re * kr - spec_im * ki
             pi = spec_re * ki + spec_im * kr
             prod = jnp.concatenate(
@@ -231,16 +232,16 @@
             @pl.loop(0, chunks)
             def _(i):
                 at = pl.ds(pl.multiple_of(i * step, 16), step)
-                e = dot(rf[i], ct[j])
+                e = dot(rf[i, 0:some * step, :], ct[j])
                 total = None if phase == 0 else acc[j, at, :]
-                for f in range(fields):
+                for f in range(some):
                     one = e[f * step:(f + 1) * step]
                     sq = one * one
                     sq = sq[:, :block] + sq[:, block:]
                     total = sq if total is None else total + sq
                 acc[j, at, :] = total
 
-            if phase == half - 1:
+            if (phase, first, some) == groups[-1]:
                 copy_s(j).start()
 
     for j in range(n_kern):

time: 72 us -> 69.1 us (0.960)
  Pallas kernels: 69.6 us -> 66.6 us
    pallas_call x1, Pallas kernels: 58.3 us -> 55.4 us  [shards(): pl.pallas_call(functools.partial(image_kernel, n_kern, n_slab), out_shape...]
where the time goes in v5:
time: 69.1 us; the launch traced here: 68.9 us
  Pallas kernels  66.6 us (96%)
  local copies, waits for them, and re-layouts  1.62 us (2%)
    pallas_call x1, Pallas kernels, shards(): pl.pallas_call(functools.partial(image_kernel, n_kern, n_slab), out_shape...  55.4 us
    pallas_call x1, Pallas kernels, shards(): pl.pallas_call(functools.partial(bake_kernel, fields * n_kern), out_shape...  11.2 us
    unnamed x8, local copies, waits for them, and re-layouts  1.62 us

profile of v5, /device:TPU:0, one launch (start us, length us, event | category | flops | bytes accessed | tf_op | source)
XLA Modules:
  0.0 68.9 jit_solution(13043882938657064064)
XLA Ops:
  0.6 0.0 copy-start.1
  0.6 0.0 copy-start.2
  0.7 0.0 copy-start.3
  0.7 55.4 %coarse_image.1.coarse_ref = f32[4,528,256]{2,1,0:T(8,128)} custom-call(s32[512,1024]{1,0:T(8,128)} %layout_hbm.1, s32[1,128]{1,0:T(1,128)} %bitcast.1, f32[2,12,128,128]{3,2,1,0:T(8,128)} %kern_hbm.1, f32[12]{0:T(128)} %eig_ref.1), custom_call_target="tpu_custom_call" | custom-call | tf_op jit(solution)/shard_map/coarse_image/pallas_call | solution.py:343
  56.1 0.0 copy-done.1
  56.1 0.0 copy-done.2
  56.1 0.0 copy-done.3
  56.1 0.0 copy-start
  56.1 1.6 %copy-done = f32[4,528,256]{2,1,0:T(8,128)S(1)} copy-done((f32[4,528,256]{2,1,0:T(8,128)S(1)}, f32[4,528,256]{2,1,0:T(8,128)}, u32[]{:S(2)}) %copy-start) | copy-done | bytes 2162712
  57.7 11.2 %interpolate_bake.1 = (f32[512,1024]{1,0:T(8,128)}, f32[512,1024]{1,0:T(8,128)}) custom-call(f32[4,528,256]{2,1,0:T(8,128)S(1)} %copy-done, bf16[1024,1152]{1,0:T(8,128)(2,1)S(1)} %copy-done.2, bf16[1024,1152]{1,0:T(8,128)(2,1)S(1)} %copy-done.1, f32[5]{0:T(128)S(1)} %copy-done.3), custom_call_target="tpu_custom_call" | custom-call | tf_op jit(solution)/shard_map/interpolate_bake/pallas_call | solution.py:377
Async XLA Ops:
  0.6 55.4 %copy-start.1 = (bf16[1024,1152]{1,0:T(8,128)(2,1)S(1)}, bf16[1024,1152]{1,0:T(8,128)(2,1)}, u32[]{:S(2)}) copy-start(bf16[1024,1152]{1,0:T(8,128)(2,1)} %constant.5.clone.dl_ref) | copy-start | bytes 7077892
  0.6 55.4 %copy-start.2 = (bf16[1024,1152]{1,0:T(8,128)(2,1)S(1)}, bf16[1024,1152]{1,0:T(8,128)(2,1)}, u32[]{:S(2)}) copy-start(bf16[1024,1152]{1,0:T(8,128)(2,1)} %constant.4.clone.dh_ref) | copy-start | bytes 7077892
  0.7 55.4 %copy-start.3 = (f32[5]{0:T(128)S(1)}, f32[5]{0:T(128)}, u32[]{:S(2)}) copy-start(f32[5]{0:T(128)} %rates_ref.1) | copy-start | bytes 64
  56.1 1.6 %copy-start = (f32[4,528,256]{2,1,0:T(8,128)S(1)}, f32[4,528,256]{2,1,0:T(8,128)}, u32[]{:S(2)}) copy-start(f32[4,528,256]{2,1,0:T(8,128)} %coarse_image.1.coarse_ref) | copy-start | bytes 6488068
